TPU v7x, 32 devices: a whole 2x2x4 slice. The times are simulated.
32 devices in a mesh: row: 4 (over y, core), col: 8 (over z, x).
Axes of the slice: x: 2, y: 2, z: 4, core: 2. Of those that a mesh axis runs over, the one named last changes fastest.
Arguments:
- features: bfloat16 [16384, 256], P(('row', 'col')), may hold values from -6 to 6
- w_self: bfloat16 [256, 256], replicated, may hold values from -0.375 to 0.375
- w_neigh: bfloat16 [256, 256], replicated, may hold values from -3 to 3
- cotangent: bfloat16 [16384, 256], P(('row', 'col')), may hold values from -6 to 6
- degree: int32 [16384], P(('row', 'col')), may hold values from 64 to 256
- tile_rows: int32 [8192], P(('row', 'col')), may hold values from 0 to 31
- tile_cols: int32 [8192], P(('row', 'col')), may hold values from 0 to 15
- tile_edges: int32 [4, 8192, 128], P(None, ('row', 'col')), may hold values from 0 to 127
- tile_count: int32 [32], P(('row', 'col')), may hold values from 4 to 256, as said below
Outputs:
- activations: bfloat16 [16384, 256], P(('row', 'col'))
- feature_grad: bfloat16 [16384, 256], P(('row', 'col'))
- grad_self: float32 [256, 256], replicated
- grad_neigh: float32 [256, 256], replicated
Inputs may be any that keep to these rules, and one draw needn't show every extreme that they name: The busiest device uses all 256 of its slots; slots from tile_count on are ignored.
All inputs are finite; a program needn't handle non-finite values.
Results may differ from a plain program's by a relative error of at most 0.0059.
Values may be sent and summed in bfloat16 or wider, within the bound.
A program may use at most 64 MiB of HBM per device.

v0:
```python
import math

import jax
import jax.numpy as jnp
from jax import lax
from jax.sharding import PartitionSpec as P


def tile_masks(edges_here, use_here):
    tile_size = edges_here.shape[2]
    matches = edges_here[:, :, :, None] == jnp.arange(tile_size, dtype=jnp.int32)
    multiplicity = jnp.sum(matches.astype(jnp.float32), axis=0)
    return (multiplicity * use_here[:, None, None]).astype(jnp.bfloat16)


def sum_weights(part_self, part_neigh):
    return lax.psum((part_self, part_neigh), ("row", "col"))


def spread_back(dscaled, row_blocks, col_blocks, edge_blocks, use_blocks, col_tile_count):
    tile_size = edge_blocks.shape[3]
    feature_dim = dscaled.shape[1]
    row_nodes = lax.all_gather(dscaled, "col", axis=0, tiled=True)
    row_tiles = row_nodes.reshape(-1, tile_size, feature_dim)

    def backward_round(running, inputs):
        rows_here, cols_here, edges_here, use_here = inputs
        pattern = tile_masks(edges_here, use_here)
        contribution = jnp.einsum(
            "bqc,bqf->bcf", pattern, row_tiles[rows_here], preferred_element_type=jnp.float32
        )
        return (running.at[cols_here].add(contribution), None)

    start_value = jnp.zeros((col_tile_count, tile_size, feature_dim), jnp.float32)
    partial_grads, _ = lax.scan(
        backward_round, start_value, (row_blocks, col_blocks, edge_blocks, use_blocks)
    )
    return lax.psum_scatter(
        partial_grads.reshape(-1, feature_dim), "row", scatter_dimension=0, tiled=True
    )


def per_device(
    features, w_self, w_neigh, cotangent, degree, tile_rows, tile_cols, tile_edges, tile_count
):
    local_rows, feature_dim = features.shape
    tile_size = tile_edges.shape[2]
    slot_count = tile_rows.shape[0]
    row_devices = lax.axis_size("row")
    col_devices = lax.axis_size("col")
    in_use = (jnp.arange(slot_count, dtype=jnp.int32) < tile_count[0]).astype(jnp.float32)
    block_size = math.gcd(slot_count, 32)
    rounds = slot_count // block_size
    edge_blocks = tile_edges.reshape(tile_edges.shape[0], rounds, block_size, tile_size).transpose(
        1, 0, 2, 3
    )
    row_blocks = tile_rows.reshape(rounds, block_size)
    col_blocks = tile_cols.reshape(rounds, block_size)
    use_blocks = in_use.reshape(rounds, block_size)
    row_tile_count = local_rows * col_devices // tile_size
    col_tile_count = local_rows * row_devices // tile_size
    column_nodes = lax.all_gather(features, "row", axis=0, tiled=True)
    column_tiles = column_nodes.reshape(-1, tile_size, feature_dim)

    def forward_round(running, inputs):
        rows_here, cols_here, edges_here, use_here = inputs
        pattern = tile_masks(edges_here, use_here)
        product = jnp.einsum(
            "bqc,bcf->bqf", pattern, column_tiles[cols_here], preferred_element_type=jnp.float32
        )
        return (running.at[rows_here].add(product), None)

    start_value = jnp.zeros((row_tile_count, tile_size, feature_dim), jnp.float32)
    partial_sums, _ = lax.scan(
        forward_round, start_value, (row_blocks, col_blocks, edge_blocks, use_blocks)
    )
    neighbour_sum = lax.psum_scatter(
        partial_sums.reshape(-1, feature_dim), "col", scatter_dimension=0, tiled=True
    )
    degree_wide = degree.astype(jnp.float32)[:, None]
    aggregate = (neighbour_sum / degree_wide).astype(jnp.bfloat16)
    preact = jnp.dot(features, w_self, preferred_element_type=jnp.float32) + jnp.dot(
        aggregate, w_neigh, preferred_element_type=jnp.float32
    )
    sigmoid_pre = jax.nn.sigmoid(preact)
    activations = (preact * sigmoid_pre).astype(jnp.bfloat16)
    slope = sigmoid_pre * (1.0 + preact * (1.0 - sigmoid_pre))
    dpreact = (cotangent.astype(jnp.float32) * slope).astype(jnp.bfloat16)
    part_self = jnp.einsum("nf,ng->fg", features, dpreact, preferred_element_type=jnp.float32)
    part_neigh = jnp.einsum("nf,ng->fg", aggregate, dpreact, preferred_element_type=jnp.float32)
    dscaled = (
        jnp.einsum("ng,fg->nf", dpreact, w_neigh, preferred_element_type=jnp.float32) / degree_wide
    ).astype(jnp.bfloat16)
    neighbour_grad = spread_back(
        dscaled, row_blocks, col_blocks, edge_blocks, use_blocks, col_tile_count
    )
    grad_pair = sum_weights(part_self, part_neigh)
    own_grad = jnp.einsum("ng,fg->nf", dpreact, w_self, preferred_element_type=jnp.float32)
    feature_grad = (own_grad + neighbour_grad).astype(jnp.bfloat16)
    total_nodes = local_rows * row_devices * col_devices
    grad_scale = 1.0 / math.sqrt(total_nodes)
    return (activations, feature_grad, grad_pair[0] * grad_scale, grad_pair[1] * grad_scale)


def solution(mesh):
    return jax.shard_map(
        per_device,
        mesh=mesh,
        in_specs=(
            P(("row", "col"), None),
            P(),
            P(),
            P(("row", "col"), None),
            P(("row", "col")),
            P(("row", "col")),
            P(("row", "col")),
            P(None, ("row", "col"), None),
            P(("row", "col")),
        ),
        out_specs=(P(("row", "col"), None), P(("row", "col"), None), P(), P()),
        check_vma=False,
    )
```

profile of v0, /device:TPU:0, one launch (start us, length us, event | category | flops | bytes accessed | tf_op | source)
XLA Modules:
  0.0 484.1 jit_solution(4418653636483678971)
XLA Ops:
  12.1 17.0 %all-gather.3.cloned.1.call-done = bf16[2048,256]{1,0:T(8,128)(2,1)} async-done(((bf16[512,256]{1,0:T(8,128)(2,1)}), bf16[2048,256]{1,0:T(8,128)(2,1)}) %all-gather.3.cloned.1.call-update) | async-done | bytes 1048592 | tf_op jit(solution)/shard_map/all_gather | solution.py:62
  31.5 135.4 %while.20 = (s32[]{:T(128)}, f32[32,128,256]{2,1,0:T(8,128)}, s32[8,32]{1,0:T(8,128)S(1)}, s32[8,4,32,128]{3,2,1,0:T(8,128)}, f32[8,32]{1,0:T(8,128)S(1)}, /*ind...) while((s32[]{:T(128)}, f32[32,128,256]{2,1,0:T(8,128)}, s32[8,32]{1,0:T(8,128)S(1)}, ...), condition=%wide.region_3.4_spmd, body=%wide.region_0.3_spmd.sunk | while | flops 276300992 | bytes 27465056 | solution.py:74
  33.1 2.9 convert_reduce_fusion.4
  38.7 9.6 %scatter_fusion = f32[32,128,256]{2,1,0:T(8,128)} fusion(f32[32,128,256]{2,1,0:T(8,128)} %get-tuple-element.261, s32[32]{0:T(128)S(1)} %get-tuple-element.241, f32[32,128,256]{2,1,0:T(8,128)} %fusion.44), kind=kCustom, calls=%fused_computation.2.clone.1 | custom fusion | flops 1048576 | bytes 12583040 | tf_op jit(solution)/shard_map/while/body/eval_jaxpr/scatter-add | solution.py:71
  50.0 2.9 convert_reduce_fusion.4
  55.6 9.7 %scatter_fusion = f32[32,128,256]{2,1,0:T(8,128)} fusion(f32[32,128,256]{2,1,0:T(8,128)} %get-tuple-element.261, s32[32]{0:T(128)S(1)} %get-tuple-element.241, f32[32,128,256]{2,1,0:T(8,128)} %fusion.44), kind=kCustom, calls=%fused_computation.2.clone.1 | custom fusion | flops 1048576 | bytes 12583040 | tf_op jit(solution)/shard_map/while/body/eval_jaxpr/scatter-add | solution.py:71
  72.6 9.7 %scatter_fusion = f32[32,128,256]{2,1,0:T(8,128)} fusion(f32[32,128,256]{2,1,0:T(8,128)} %get-tuple-element.261, s32[32]{0:T(128)S(1)} %get-tuple-element.241, f32[32,128,256]{2,1,0:T(8,128)} %fusion.44), kind=kCustom, calls=%fused_computation.2.clone.1 | custom fusion | flops 1048576 | bytes 12583040 | tf_op jit(solution)/shard_map/while/body/eval_jaxpr/scatter-add | solution.py:71
  89.6 9.7 %scatter_fusion = f32[32,128,256]{2,1,0:T(8,128)} fusion(f32[32,128,256]{2,1,0:T(8,128)} %get-tuple-element.261, s32[32]{0:T(128)S(1)} %get-tuple-element.241, f32[32,128,256]{2,1,0:T(8,128)} %fusion.44), kind=kCustom, calls=%fused_computation.2.clone.1 | custom fusion | flops 1048576 | bytes 12583040 | tf_op jit(solution)/shard_map/while/body/eval_jaxpr/scatter-add | solution.py:71
  106.6 9.7 %scatter_fusion = f32[32,128,256]{2,1,0:T(8,128)} fusion(f32[32,128,256]{2,1,0:T(8,128)} %get-tuple-element.261, s32[32]{0:T(128)S(1)} %get-tuple-element.241, f32[32,128,256]{2,1,0:T(8,128)} %fusion.44), kind=kCustom, calls=%fused_computation.2.clone.1 | custom fusion | flops 1048576 | bytes 12583040 | tf_op jit(solution)/shard_map/while/body/eval_jaxpr/scatter-add | solution.py:71
  123.6 9.7 %scatter_fusion = f32[32,128,256]{2,1,0:T(8,128)} fusion(f32[32,128,256]{2,1,0:T(8,128)} %get-tuple-element.261, s32[32]{0:T(128)S(1)} %get-tuple-element.241, f32[32,128,256]{2,1,0:T(8,128)} %fusion.44), kind=kCustom, calls=%fused_computation.2.clone.1 | custom fusion | flops 1048576 | bytes 12583040 | tf_op jit(solution)/shard_map/while/body/eval_jaxpr/scatter-add | solution.py:71
  140.5 9.6 %scatter_fusion = f32[32,128,256]{2,1,0:T(8,128)} fusion(f32[32,128,256]{2,1,0:T(8,128)} %get-tuple-element.261, s32[32]{0:T(128)S(1)} %get-tuple-element.241, f32[32,128,256]{2,1,0:T(8,128)} %fusion.44), kind=kCustom, calls=%fused_computation.2.clone.1 | custom fusion | flops 1048576 | bytes 12583040 | tf_op jit(solution)/shard_map/while/body/eval_jaxpr/scatter-add | solution.py:71
  157.4 9.6 %scatter_fusion = f32[32,128,256]{2,1,0:T(8,128)} fusion(f32[32,128,256]{2,1,0:T(8,128)} %get-tuple-element.261, s32[32]{0:T(128)S(1)} %get-tuple-element.241, f32[32,128,256]{2,1,0:T(8,128)} %fusion.44), kind=kCustom, calls=%fused_computation.2.clone.1 | custom fusion | flops 1048576 | bytes 12583040 | tf_op jit(solution)/shard_map/while/body/eval_jaxpr/scatter-add | solution.py:71
  168.2 87.2 %reduce-scatter.3.cloned.1.call-done = f32[512,256]{1,0:T(8,128)} async-done(((f32[4096,256]{1,0:T(8,128)}), f32[512,256]{1,0:T(8,128)}) %reduce-scatter.3.cloned.1.call-update) | async-done | bytes 524304 | tf_op jit(solution)/shard_map/reduce_scatter | solution.py:77
  260.8 47.1 %all-gather.5.cloned.1.call-done = bf16[4096,256]{1,0:T(8,128)(2,1)} async-done(((bf16[512,256]{1,0:T(8,128)(2,1)}), bf16[4096,256]{1,0:T(8,128)(2,1)}) %all-gather.5.cloned.1.call-update) | async-done | bytes 2097168 | tf_op jit(solution)/shard_map/all_gather | solution.py:23
  308.1 135.9 %while.21 = (s32[]{:T(128)}, f32[16,128,256]{2,1,0:T(8,128)S(1)}, s32[8,32]{1,0:T(8,128)S(1)}, s32[8,4,32,128]{3,2,1,0:T(8,128)}, f32[8,32]{1,0:T(8,128)S(1)}, /...) while((s32[]{:T(128)}, f32[16,128,256]{2,1,0:T(8,128)S(1)}, s32[8,32]{1,0:T(8,128)S(1)}, ...), condition=%wide.region_8.9_spmd, body=%wide.region_5.8_spmd.sunk | while | flops 276300992 | bytes 35853692 | solution.py:35
  308.2 3.6 gather_fusion.1
  318.6 6.5 %scatter_fusion.1 = f32[16,128,256]{2,1,0:T(8,128)S(1)} fusion(f32[16,128,256]{2,1,0:T(8,128)S(1)} %get-tuple-element.285, s32[32]{0:T(128)S(1)} %get-tuple-element.250, f32[32,128,256]{2,1,0:T(8,128)} %fusion.48), kind=kCustom, calls=%fused_computation.3.clone.1 | custom fusion | flops 1048576 | bytes 12583040 | tf_op jit(solution)/shard_map/while/body/eval_jaxpr/scatter-add | solution.py:32
  325.2 3.6 gather_fusion.1
  335.6 6.5 %scatter_fusion.1 = f32[16,128,256]{2,1,0:T(8,128)S(1)} fusion(f32[16,128,256]{2,1,0:T(8,128)S(1)} %get-tuple-element.285, s32[32]{0:T(128)S(1)} %get-tuple-element.250, f32[32,128,256]{2,1,0:T(8,128)} %fusion.48), kind=kCustom, calls=%fused_computation.3.clone.1 | custom fusion | flops 1048576 | bytes 12583040 | tf_op jit(solution)/shard_map/while/body/eval_jaxpr/scatter-add | solution.py:32
  342.2 3.6 gather_fusion.1
  352.6 6.5 %scatter_fusion.1 = f32[16,128,256]{2,1,0:T(8,128)S(1)} fusion(f32[16,128,256]{2,1,0:T(8,128)S(1)} %get-tuple-element.285, s32[32]{0:T(128)S(1)} %get-tuple-element.250, f32[32,128,256]{2,1,0:T(8,128)} %fusion.48), kind=kCustom, calls=%fused_computation.3.clone.1 | custom fusion | flops 1048576 | bytes 12583040 | tf_op jit(solution)/shard_map/while/body/eval_jaxpr/scatter-add | solution.py:32
  359.2 3.6 gather_fusion.1
  369.6 6.5 %scatter_fusion.1 = f32[16,128,256]{2,1,0:T(8,128)S(1)} fusion(f32[16,128,256]{2,1,0:T(8,128)S(1)} %get-tuple-element.285, s32[32]{0:T(128)S(1)} %get-tuple-element.250, f32[32,128,256]{2,1,0:T(8,128)} %fusion.48), kind=kCustom, calls=%fused_computation.3.clone.1 | custom fusion | flops 1048576 | bytes 12583040 | tf_op jit(solution)/shard_map/while/body/eval_jaxpr/scatter-add | solution.py:32
  376.2 3.6 gather_fusion.1
  386.6 6.5 %scatter_fusion.1 = f32[16,128,256]{2,1,0:T(8,128)S(1)} fusion(f32[16,128,256]{2,1,0:T(8,128)S(1)} %get-tuple-element.285, s32[32]{0:T(128)S(1)} %get-tuple-element.250, f32[32,128,256]{2,1,0:T(8,128)} %fusion.48), kind=kCustom, calls=%fused_computation.3.clone.1 | custom fusion | flops 1048576 | bytes 12583040 | tf_op jit(solution)/shard_map/while/body/eval_jaxpr/scatter-add | solution.py:32
  393.2 3.6 gather_fusion.1
  403.6 6.5 %scatter_fusion.1 = f32[16,128,256]{2,1,0:T(8,128)S(1)} fusion(f32[16,128,256]{2,1,0:T(8,128)S(1)} %get-tuple-element.285, s32[32]{0:T(128)S(1)} %get-tuple-element.250, f32[32,128,256]{2,1,0:T(8,128)} %fusion.48), kind=kCustom, calls=%fused_computation.3.clone.1 | custom fusion | flops 1048576 | bytes 12583040 | tf_op jit(solution)/shard_map/while/body/eval_jaxpr/scatter-add | solution.py:32
  410.1 3.6 gather_fusion.1
  420.6 6.5 %scatter_fusion.1 = f32[16,128,256]{2,1,0:T(8,128)S(1)} fusion(f32[16,128,256]{2,1,0:T(8,128)S(1)} %get-tuple-element.285, s32[32]{0:T(128)S(1)} %get-tuple-element.250, f32[32,128,256]{2,1,0:T(8,128)} %fusion.48), kind=kCustom, calls=%fused_computation.3.clone.1 | custom fusion | flops 1048576 | bytes 12583040 | tf_op jit(solution)/shard_map/while/body/eval_jaxpr/scatter-add | solution.py:32
  427.1 3.6 gather_fusion.1
  437.6 6.5 %scatter_fusion.1 = f32[16,128,256]{2,1,0:T(8,128)S(1)} fusion(f32[16,128,256]{2,1,0:T(8,128)S(1)} %get-tuple-element.285, s32[32]{0:T(128)S(1)} %get-tuple-element.250, f32[32,128,256]{2,1,0:T(8,128)} %fusion.48), kind=kCustom, calls=%fused_computation.3.clone.1 | custom fusion | flops 1048576 | bytes 12583040 | tf_op jit(solution)/shard_map/while/body/eval_jaxpr/scatter-add | solution.py:32
  448.2 27.3 %reduce-scatter.5.cloned.1.call-done = f32[512,256]{1,0:T(8,128)} async-done(((f32[2048,256]{1,0:T(8,128)}), f32[512,256]{1,0:T(8,128)}) %reduce-scatter.5.cloned.1.call-update) | async-done | bytes 524304 | tf_op jit(solution)/shard_map/reduce_scatter | solution.py:38
  (160 shorter events, 126.1 us)
Async XLA Ops:
  7.2 249.4 %copy-start = (bf16[256,256]{1,0:T(8,128)(2,1)S(1)}, bf16[256,256]{1,0:T(8,128)(2,1)}, u32[]{:S(2)}) copy-start(bf16[256,256]{1,0:T(8,128)(2,1)} %param.15) | copy-start | bytes 393220
  7.2 21.9 %all-gather.3.cloned.1.call-start = ((), (), s32[]{:S(2)}) async-start(), calls=%async_computation.2 | async-start | bytes 1310720 | tf_op jit(solution)/shard_map/all_gather | solution.py:62
  7.9 247.5 %reduce-scatter.3.cloned.1.call-start = ((), (), s32[]{:S(2)}) async-start(), calls=%async_computation.3 | async-start | bytes 4718592 | tf_op jit(solution)/shard_map/reduce_scatter | solution.py:77
  29.0 2.5 copy-start.3
  166.9 0.7 copy-start.6
  166.9 1.0 copy-start.4
  166.9 1.0 copy-start.5
  166.9 89.7 %copy-start.7 = (bf16[512,256]{1,0:T(8,128)(2,1)S(1)}, bf16[512,256]{1,0:T(8,128)(2,1)}, u32[]{:S(2)}) copy-start(bf16[512,256]{1,0:T(8,128)(2,1)} %param.16) | copy-start | bytes 786436
  167.0 141.0 %all-gather.5.cloned.1.call-start = ((), (), s32[]{:S(2)}) async-start(), calls=%async_computation.4 | async-start | bytes 2359296 | tf_op jit(solution)/shard_map/all_gather | solution.py:23
  258.7 186.7 %all-reduce.3.cloned.1.call-start = ((), (), s32[]{:S(2)}) async-start(), calls=%async_computation.6 | async-start | bytes 1048576 | tf_op jit(solution)/shard_map/psum | solution.py:17
  260.7 214.8 %reduce-scatter.5.cloned.1.call-start = ((), (), s32[]{:S(2)}) async-start(), calls=%async_computation.5 | async-start | bytes 2621440 | tf_op jit(solution)/shard_map/reduce_scatter | solution.py:38
  311.8 4.0 copy-start.2
  328.8 4.0 copy-start.2
  345.8 4.0 copy-start.2
  362.8 4.0 copy-start.2
  379.8 4.0 copy-start.2
  396.8 4.0 copy-start.2
  413.8 4.0 copy-start.2
  430.7 4.0 copy-start.2
  444.1 1.3 copy-start.1
Sparse Core Ops, SparseCore 0:
  9.6 19.4 all-gather.2
  167.1 88.2 reduce-scatter.2
  258.8 49.0 all-gather.4
  314.7 126.5 all-reduce.2
  445.6 29.9 reduce-scatter.4
where the time goes:
time: 486 us; the launch traced here: 484 us
  waiting for transfers between devices  179 us (37%)
  other arithmetic  179 us (37%)
  local copies, waits for them, and re-layouts  59.3 us (12%)
  matrix products  51.2 us (11%)
  between operations  14.5 us (3%)
    reduce_scatter x1, waiting for transfers between devices, per_device(): lax.psum_scatter(partial_sums.reshape(-1, feature_dim), 'col', scatter_di...  87.2 us
    scatter-add x8, other arithmetic, forward_round(): return (running.at[rows_here].add(product), None)  77.5 us
    scatter-add x8, other arithmetic, backward_round(): return (running.at[cols_here].add(contribution), None)  51.9 us
    all_gather x1, waiting for transfers between devices, spread_back(): row_nodes = lax.all_gather(dscaled, 'col', axis=0, tiled=True)  47.1 us
    reduce_sum x16, other arithmetic, tile_masks(): multiplicity = jnp.sum(matches.astype(jnp.float32), axis=0)  46.8 us
    gather x8, local copies, waits for them, and re-layouts, backward_round(): row_tiles[rows_here]  28.9 us
    reduce_scatter x1, waiting for transfers between devices, spread_back(): lax.psum_scatter(partial_grads.reshape(-1, feature_dim), 'row', scatter_d...  27.3 us
    dot_general x8, matrix products, backward_round(): jnp.einsum('bqc,bqf->bcf', pattern, row_tiles[rows_here], preferred_eleme...  23.1 us
  transfers between devices with their start and end apart: 5, of which 4 were waited for; matrix products, arithmetic and copies ran while one was open for 30% of the time, Pallas kernels for 0%

commit v1 on v0

v1 whole, which is shorter than its diff:
```python
import functools
import math

import jax
import jax.numpy as jnp
from jax import lax
from jax.experimental import pallas as pl
from jax.experimental.pallas import tpu as pltpu
from jax.sharding import PartitionSpec as P

VMEM_LIMIT = 48 * 1024 * 1024
UNROLL = 8
UNUSED = 255


class Copies:
    def __init__(self, send_sems):
        self.send_sems = send_sems
        self.started = []

    def send(self, src, dst, recv_sem, device, cond=None):
        copy = pltpu.make_async_remote_copy(
            src_ref=src,
            dst_ref=dst,
            send_sem=self.send_sems.at[len(self.started)],
            recv_sem=recv_sem,
            device_id=device,
            device_id_type=pl.DeviceIdType.MESH,
        )
        self.started.append((cond, copy))
        if cond is None:
            copy.start()
        else:
            pl.when(cond)(lambda: copy.start())

    def wait_recv(self, dst, recv_sem, device):
        pltpu.make_async_remote_copy(
            src_ref=dst,
            dst_ref=dst,
            send_sem=self.send_sems.at[0],
            recv_sem=recv_sem,
            device_id=device,
            device_id_type=pl.DeviceIdType.MESH,
        ).wait_recv()

    def finish(self):
        for cond, copy in self.started:
            if cond is None:
                copy.wait_send()
            else:
                pl.when(cond)(lambda copy=copy: copy.wait_send())


def signal(device):
    pl.semaphore_signal(
        pltpu.get_barrier_semaphore(),
        inc=1,
        device_id=device,
        device_id_type=pl.DeviceIdType.MESH,
    )


def both(x, y):
    return jnp.logical_and(x, y)


def gather_rows_kernel(n_row, own_ref, out_ref, send_sems, recv_sems, local_sem):
    groups = n_row // 2
    half = own_ref.shape[0] // 2
    me = lax.axis_index("row")
    place = me // 2
    core = me % 2
    sibling = {"row": place * 2 + (1 - core)}
    peers = [{"row": lax.rem(place + k, groups) * 2 + core} for k in range(1, groups)]
    for device in [sibling] + peers:
        signal(device)
    keep = pltpu.make_async_copy(own_ref, out_ref.at[me], local_sem)
    keep.start()
    pl.semaphore_wait(pltpu.get_barrier_semaphore(), groups)
    copies = Copies(send_sems)
    for part in range(2):
        rows = pl.ds(part * half, half)
        for device in peers + [sibling]:
            copies.send(
                own_ref.at[rows], out_ref.at[me, rows], recv_sems.at[me, part], device
            )
    for part in range(2):
        rows = pl.ds(part * half, half)
        for k in range(1, groups):
            source = lax.rem(place + groups - k, groups) * 2 + core
            block = out_ref.at[source, rows]
            copies.wait_recv(block, recv_sems.at[source, part], sibling)
            copies.send(block, block, recv_sems.at[source, part], sibling)
    for part in range(2):
        rows = pl.ds(part * half, half)
        for k in range(groups):
            source = lax.rem(place + groups - k, groups) * 2 + (1 - core)
            copies.wait_recv(out_ref.at[source, rows], recv_sems.at[source, part], sibling)
    keep.wait()
    copies.finish()


def gather_rows(features, n_row):
    rows, width = features.shape
    return pl.pallas_call(
        functools.partial(gather_rows_kernel, n_row),
        out_shape=jax.ShapeDtypeStruct((n_row, rows, width), features.dtype),
        in_specs=[pl.BlockSpec(memory_space=pltpu.VMEM)],
        out_specs=pl.BlockSpec(memory_space=pltpu.VMEM),
        scratch_shapes=[
            pltpu.SemaphoreType.DMA((4 * n_row,)),
            pltpu.SemaphoreType.DMA((n_row, 2)),
            pltpu.SemaphoreType.DMA,
        ],
        compiler_params=pltpu.CompilerParams(
            collective_id=0, has_side_effects=True, vmem_limit_bytes=VMEM_LIMIT
        ),
        name="gather_rows",
    )(features)


def spread_kernel(
    forward, rows_ref, cols_ref, count_ref, edges_ref, nodes_ref, out_ref, acc_ref
):
    tile = edges_ref.shape[2]
    edge_count = edges_ref.shape[0]
    acc_ref[...] = jnp.zeros_like(acc_ref)
    column = (
        lax.broadcasted_iota(jnp.int32, (tile // 16, 16, tile), 0) * 16
        + lax.broadcasted_iota(jnp.int32, (tile // 16, 16, tile), 1)
    ).astype(jnp.float32).astype(jnp.bfloat16)
    one = jnp.ones(column.shape, jnp.bfloat16)
    zero = jnp.zeros(column.shape, jnp.bfloat16)

    def pattern(slot):
        total = None
        for k in range(edge_count):
            row = edges_ref[k, pl.ds(slot, 1), :]
            wide = jnp.broadcast_to(row, (16, tile)).astype(jnp.float32).astype(jnp.bfloat16)
            hit = jnp.where(wide[None] == column, one, zero)
            total = hit if total is None else total + hit
        return total.reshape(tile, tile)

    def body(step, carry):
        first = step * UNROLL
        products = []
        for u in range(UNROLL):
            slot = first + u
            if forward:
                products.append(
                    lax.dot_general(
                        pattern(slot),
                        nodes_ref[cols_ref[slot]],
                        (((0,), (0,)), ((), ())),
                        preferred_element_type=jnp.float32,
                    )
                )
            else:
                products.append(
                    jnp.dot(
                        pattern(slot),
                        nodes_ref[rows_ref[slot]],
                        preferred_element_type=jnp.float32,
                    )
                )
        for u in range(UNROLL):
            slot = first + u
            target = rows_ref[slot] if forward else cols_ref[slot]
            acc_ref[target] += products[u]
        return carry

    steps = lax.div(count_ref[0] + (UNROLL - 1), UNROLL)
    lax.fori_loop(0, steps, body, 0)

    def finish(index, carry):
        out_ref[index] = acc_ref[index].astype(out_ref.dtype)
        return carry

    lax.fori_loop(0, out_ref.shape[0], finish, 0)


def spread(forward, tile_rows, tile_cols, tile_count, edges, nodes, out_tiles):
    tile = edges.shape[2]
    width = nodes.shape[-1]
    node_tiles = nodes.reshape(-1, tile, width)
    smem = pl.BlockSpec(memory_space=pltpu.SMEM)
    vmem = pl.BlockSpec(memory_space=pltpu.VMEM)
    return pl.pallas_call(
        functools.partial(spread_kernel, forward),
        out_shape=jax.ShapeDtypeStruct((out_tiles, tile, width), jnp.bfloat16),
        in_specs=[smem, smem, smem, vmem, vmem],
        out_specs=vmem,
        scratch_shapes=[pltpu.VMEM((out_tiles, tile, width), jnp.float32)],
        compiler_params=pltpu.CompilerParams(vmem_limit_bytes=VMEM_LIMIT),
        cost_estimate=pl.CostEstimate(
            flops=2 * edges.shape[1] * tile * tile * width,
            bytes_accessed=edges.size * 4 + nodes.size * 2 + out_tiles * tile * width * 2,
            transcendentals=0,
        ),
        name="spread_forward" if forward else "spread_back",
    )(tile_rows, tile_cols, tile_count, edges, node_tiles)


def layer_kernel(
    far,
    near,
    part_ref,
    feat_ref,
    w_self_ref,
    w_neigh_ref,
    cot_ref,
    degree_ref,
    act_ref,
    own_ref,
    grads_ref,
    all_ref,
    below_a,
    above_a,
    below_b,
    above_b,
    cross_a,
    cross_b,
    stage_a,
    stage_b,
    total,
    tmp,
    agg,
    dpre,
    send_sems,
    below_a_sems,
    above_a_sems,
    below_b_sems,
    above_b_sems,
    cross_a_sems,
    cross_b_sems,
    gather_sems,
):
    f32, bf16 = jnp.float32, jnp.bfloat16
    rows, width = feat_ref.shape
    half = rows // 2
    upper, lower = pl.ds(0, half), pl.ds(half, half)
    me = lax.axis_index("col")
    a = me // near
    b = me % near

    def at(a_index, b_index):
        return {"col": a_index * near + b_index}

    has_below, has_above = a > 0, a < far - 1
    below, above = at(a - 1, b), at(a + 1, b)
    ahead = [lax.rem(b + k, near) for k in range(1, near)]
    behind = [lax.rem(b + near - k, near) for k in range(1, near)]
    any_peer = at(a, ahead[0]) if near > 1 else at(lax.rem(a + 1, far), b)

    for other in ahead:
        signal(at(a, other))
    pl.when(has_below)(lambda: signal(below))
    pl.when(has_above)(lambda: signal(above))
    greeted = near - 1 + has_below.astype(jnp.int32) + has_above.astype(jnp.int32)
    pl.semaphore_wait(pltpu.get_barrier_semaphore(), greeted)

    copies = Copies(send_sems)
    up = (1, above, has_below, below_a, below_a_sems, below_b, below_b_sems)
    down = (-1, below, has_above, above_a, above_a_sems, above_b, above_b_sems)

    def reached(index):
        return both(index >= 0, index < far)

    for d in range(far - 1, -1, -1):
        for sign in (1, -1) if d else (1,):
            dest = a + sign * d
            for k in range(1, near):
                copies.send(
                    part_ref.at[dest * near + ahead[k - 1], lower],
                    cross_b.at[k - 1, dest],
                    cross_b_sems.at[k - 1, dest],
                    at(a, ahead[k - 1]),
                    reached(dest) if d else None,
                )
    for d in range(far - 1, 0, -1):
        for sign, onward, arrives, got_a, got_a_sems, got_b, got_b_sems in (up, down):
            dest = a + sign * d
            valid = reached(dest)
            for b_index in range(near):
                j = dest * near + b_index

                @pl.when(both(valid, arrives))
                def _():
                    copies.wait_recv(got_a.at[j], got_a_sems.at[j], any_peer)
                    stage_a[j] = (
                        part_ref[j, upper].astype(f32) + got_a[j].astype(f32)
                    ).astype(bf16)

                @pl.when(both(valid, jnp.logical_not(arrives)))
                def _():
                    stage_a[j] = part_ref[j, upper]

                copies.send(stage_a.at[j], got_a.at[j], got_a_sems.at[j], onward, valid)
        for sign, onward, arrives, got_a, got_a_sems, got_b, got_b_sems in (up, down):
            dest = a + sign * d
            valid = reached(dest)

            @pl.when(valid)
            def _():
                value = part_ref[dest * near + b, lower].astype(f32)
                for k in range(1, near):
                    copies.wait_recv(
                        cross_b.at[k - 1, dest], cross_b_sems.at[k - 1, dest], any_peer
                    )
                    value = value + cross_b[k - 1, dest].astype(f32)
                tmp[...] = value

            @pl.when(both(valid, arrives))
            def _():
                copies.wait_recv(got_b.at[dest], got_b_sems.at[dest], any_peer)
                tmp[...] += got_b[dest].astype(f32)

            @pl.when(valid)
            def _():
                stage_b[dest] = tmp[...].astype(bf16)

            copies.send(stage_b.at[dest], got_b.at[dest], got_b_sems.at[dest], onward, valid)

    def add_both(ref, window, arrived_below, below_sem, arrived_above, above_sem):
        @pl.when(has_below)
        def _():
            copies.wait_recv(arrived_below, below_sem, any_peer)
            ref[window] += arrived_below[...].astype(f32)

        @pl.when(has_above)
        def _():
            copies.wait_recv(arrived_above, above_sem, any_peer)
            ref[window] += arrived_above[...].astype(f32)

    whole = pl.ds(0, half)
    for k in range(1, near):
        j = a * near + ahead[k - 1]
        tmp[...] = part_ref[j, upper].astype(f32)
        add_both(tmp, whole, below_a.at[j], below_a_sems.at[j], above_a.at[j], above_a_sems.at[j])
        stage_a[j] = tmp[...].astype(bf16)
        copies.send(
            stage_a.at[j], cross_a.at[k - 1], cross_a_sems.at[k - 1], at(a, ahead[k - 1])
        )
    total[upper] = part_ref[me, upper].astype(f32)
    add_both(
        total, upper, below_a.at[me], below_a_sems.at[me], above_a.at[me], above_a_sems.at[me]
    )
    total[lower] = part_ref[me, lower].astype(f32)
    for k in range(1, near):
        copies.wait_recv(cross_b.at[k - 1, a], cross_b_sems.at[k - 1, a], any_peer)
        total[lower] += cross_b[k - 1, a].astype(f32)
    add_both(
        total, lower, below_b.at[a], below_b_sems.at[a], above_b.at[a], above_b_sems.at[a]
    )

    def layer(window):
        degree = degree_ref[window]
        aggregate = (total[window] / degree).astype(bf16)
        agg[window] = aggregate
        preact = jnp.dot(
            feat_ref[window], w_self_ref[...], preferred_element_type=f32
        ) + jnp.dot(aggregate, w_neigh_ref[...], preferred_element_type=f32)
        gate = jax.nn.sigmoid(preact)
        act_ref[window] = (preact * gate).astype(bf16)
        slope = gate * (1.0 + preact * (1.0 - gate))
        dpreact = (cot_ref[window].astype(f32) * slope).astype(bf16)
        dpre[window] = dpreact
        back = lax.dot_general(
            dpreact, w_neigh_ref[...], (((1,), (1,)), ((), ())), preferred_element_type=f32
        )
        all_ref[me, window] = (back / degree).astype(bf16)

    def hand_on(j, window, part, device, cond=None):
        copies.send(
            all_ref.at[j, window], all_ref.at[j, window], gather_sems.at[part, j], device, cond
        )

    def arrive(j, window, part):
        copies.wait_recv(all_ref.at[j, window], gather_sems.at[part, j], any_peer)

    layer(lower)
    hand_on(me, lower, 1, above, has_above)
    hand_on(me, lower, 1, below, has_below)
    for other in ahead:
        hand_on(me, lower, 1, at(a, other))
    for k in range(1, near):
        copies.wait_recv(cross_a.at[k - 1], cross_a_sems.at[k - 1], any_peer)
        total[upper] += cross_a[k - 1].astype(f32)
    layer(upper)
    for other in ahead:
        hand_on(me, upper, 0, at(a, other))
    hand_on(me, upper, 0, above, has_above)
    hand_on(me, upper, 0, below, has_below)

    contract_rows = (((0,), (0,)), ((), ()))
    grads_ref[0] = lax.dot_general(
        feat_ref[...], dpre[...], contract_rows, preferred_element_type=f32
    )
    grads_ref[1] = lax.dot_general(
        agg[...], dpre[...], contract_rows, preferred_element_type=f32
    )
    for other in behind:
        j = a * near + other
        arrive(j, upper, 0)
        hand_on(j, upper, 0, above, has_above)
        hand_on(j, upper, 0, below, has_below)
    own_ref[...] = lax.dot_general(
        dpre[...], w_self_ref[...], (((1,), (1,)), ((), ())), preferred_element_type=f32
    )
    sides = ((1, above, has_above), (-1, below, has_below))
    for d in range(1, far):
        for sign, onward, goes_on in sides:
            source = a - sign * d
            valid = reached(source)
            j = source * near + b
            pl.when(valid)(lambda: arrive(j, lower, 1))
            hand_on(j, lower, 1, onward, both(valid, goes_on))
            for other in ahead:
                hand_on(j, lower, 1, at(a, other), valid)
        for sign, onward, goes_on in sides:
            source = a - sign * d
            valid = reached(source)
            for b_index in range(near):
                j = source * near + b_index
                pl.when(valid)(lambda: arrive(j, upper, 0))
                hand_on(j, upper, 0, onward, both(valid, goes_on))
    for a_index in range(far):
        for other in behind:
            arrive(a_index * near + other, lower, 1)
    copies.finish()


def layer_call(partials, features, w_self, w_neigh, cotangent, degree, n_col):
    far = 4 if n_col % 4 == 0 else n_col
    near = n_col // far
    rows, width = features.shape
    half = rows // 2
    bf16, f32 = jnp.bfloat16, jnp.float32
    vmem = pl.BlockSpec(memory_space=pltpu.VMEM)
    crosses = max(near - 1, 1)
    dma = pltpu.SemaphoreType.DMA
    return pl.pallas_call(
        functools.partial(layer_kernel, far, near),
        out_shape=(
            jax.ShapeDtypeStruct((rows, width), bf16),
            jax.ShapeDtypeStruct((rows, width), f32),
            jax.ShapeDtypeStruct((2, width, width), f32),
            jax.ShapeDtypeStruct((n_col, rows, width), bf16),
        ),
        in_specs=[vmem] * 6,
        out_specs=(vmem,) * 4,
        scratch_shapes=[
            pltpu.VMEM((n_col, half, width), bf16),
            pltpu.VMEM((n_col, half, width), bf16),
            pltpu.VMEM((far, half, width), bf16),
            pltpu.VMEM((far, half, width), bf16),
            pltpu.VMEM((crosses, half, width), bf16),
            pltpu.VMEM((crosses, far, half, width), bf16),
            pltpu.VMEM((n_col, half, width), bf16),
            pltpu.VMEM((far, half, width), bf16),
            pltpu.VMEM((rows, width), f32),
            pltpu.VMEM((half, width), f32),
            pltpu.VMEM((rows, width), bf16),
            pltpu.VMEM((rows, width), bf16),
            dma((16 * n_col,)),
            dma((n_col,)),
            dma((n_col,)),
            dma((far,)),
            dma((far,)),
            dma((crosses,)),
            dma((crosses, far)),
            dma((2, n_col)),
        ],
        compiler_params=pltpu.CompilerParams(
            collective_id=1, has_side_effects=True, vmem_limit_bytes=VMEM_LIMIT
        ),
        name="layer",
    )(partials, features, w_self, w_neigh, cotangent, degree)


def scatter_rows_kernel(
    n_row, part_ref, own_ref, out_ref, from_sibling, staged, from_peer, total, send_sems,
    sibling_sems, peer_sems,
):
    f32 = jnp.float32
    groups = n_row // 2
    half = own_ref.shape[0] // 2
    me = lax.axis_index("row")
    place = me // 2
    core = me % 2
    sibling = {"row": place * 2 + (1 - core)}
    peers = [lax.rem(place + k, groups) for k in range(1, groups)]
    for device in [sibling] + [{"row": peer * 2 + core} for peer in peers]:
        signal(device)
    pl.semaphore_wait(pltpu.get_barrier_semaphore(), groups)
    copies = Copies(send_sems)
    windows = [pl.ds(part * half, half) for part in range(2)]
    for peer in peers + [place]:
        for part, rows in enumerate(windows):
            copies.send(
                part_ref.at[peer * 2 + (1 - core), rows],
                from_sibling.at[peer, rows],
                sibling_sems.at[peer, part],
                sibling,
            )
    for k, peer in enumerate(peers):
        for part, rows in enumerate(windows):
            copies.wait_recv(from_sibling.at[peer, rows], sibling_sems.at[peer, part], sibling)
            staged[k, rows] = (
                part_ref[peer * 2 + core, rows].astype(f32)
                + from_sibling[peer, rows].astype(f32)
            ).astype(staged.dtype)
            copies.send(
                staged.at[k, rows],
                from_peer.at[k, rows],
                peer_sems.at[k, part],
                {"row": peer * 2 + core},
            )
    for part, rows in enumerate(windows):
        copies.wait_recv(from_sibling.at[place, rows], sibling_sems.at[place, part], sibling)
        total[rows] = (
            own_ref[rows]
            + part_ref[me, rows].astype(f32)
            + from_sibling[place, rows].astype(f32)
        )
    for part, rows in enumerate(windows):
        value = total[rows]
        for k in range(groups - 1):
            copies.wait_recv(from_peer.at[k, rows], peer_sems.at[k, part], sibling)
            value = value + from_peer[k, rows].astype(f32)
        out_ref[rows] = value.astype(out_ref.dtype)
    copies.finish()


def scatter_rows(partials, own_grad, n_row):
    rows, width = own_grad.shape
    groups = n_row // 2
    others = max(groups - 1, 1)
    vmem = pl.BlockSpec(memory_space=pltpu.VMEM)
    bf16 = jnp.bfloat16
    dma = pltpu.SemaphoreType.DMA
    return pl.pallas_call(
        functools.partial(scatter_rows_kernel, n_row),
        out_shape=jax.ShapeDtypeStruct((rows, width), bf16),
        in_specs=[vmem] * 2,
        out_specs=vmem,
        scratch_shapes=[
            pltpu.VMEM((groups, rows, width), bf16),
            pltpu.VMEM((others, rows, width), bf16),
            pltpu.VMEM((others, rows, width), bf16),
            pltpu.VMEM((rows, width), jnp.float32),
            dma((4 * groups,)),
            dma((groups, 2)),
            dma((others, 2)),
        ],
        compiler_params=pltpu.CompilerParams(
            collective_id=2, has_side_effects=True, vmem_limit_bytes=VMEM_LIMIT
        ),
        name="scatter_rows",
    )(partials, own_grad)


def per_device(
    features, w_self, w_neigh, cotangent, degree, tile_rows, tile_cols, tile_edges, tile_count
):
    rows, width = features.shape
    tile = tile_edges.shape[2]
    slots = tile_rows.shape[0]
    n_row = lax.axis_size("row")
    n_col = lax.axis_size("col")
    in_use = jnp.arange(slots, dtype=jnp.int32) < tile_count[0]
    edges = jnp.where(in_use[None, :, None], tile_edges, UNUSED)
    padding = (-slots) % UNROLL
    if padding:
        edges = jnp.pad(edges, ((0, 0), (0, padding), (0, 0)), constant_values=UNUSED)
        tile_rows = jnp.pad(tile_rows, (0, padding))
        tile_cols = jnp.pad(tile_cols, (0, padding))
    degree_wide = degree.astype(jnp.float32)[:, None]

    column_nodes = gather_rows(features, n_row)
    partial_sums = spread(
        True, tile_rows, tile_cols, tile_count, edges, column_nodes, rows * n_col // tile
    )
    activations, own_grad, grads, row_nodes = layer_call(
        partial_sums.reshape(n_col, rows, width),
        features,
        w_self,
        w_neigh,
        cotangent,
        degree_wide,
        n_col,
    )
    partial_grads = spread(
        False, tile_rows, tile_cols, tile_count, edges, row_nodes, rows * n_row // tile
    )
    grads = lax.psum(grads, ("row", "col")) * (1.0 / math.sqrt(rows * n_row * n_col))
    feature_grad = scatter_rows(partial_grads.reshape(n_row, rows, width), own_grad, n_row)
    return (activations, feature_grad, grads[0], grads[1])


def solution(mesh):
    nodes = P(("row", "col"), None)
    flat = P(("row", "col"))
    return jax.shard_map(
        per_device,
        mesh=mesh,
        in_specs=(nodes, P(), P(), nodes, flat, flat, flat, P(None, ("row", "col"), None), flat),
        out_specs=(nodes, nodes, P(), P()),
        check_vma=False,
    )
```

time: 486 us -> 234 us (0.48)
  other arithmetic: 179 us -> 2.92 us
  Pallas kernels: 0 us -> 105 us
  waiting for transfers between devices: 179 us -> 103 us
  local copies, waits for them, and re-layouts: 59.3 us -> 7.59 us
  matrix products: 51.2 us -> 0 us
    scatter-add x16 -> x0, other arithmetic: 129 us -> none  [the longest x8 77.5 us: forward_round(): return (running.at[rows_here].add(product), None)]
    reduce_scatter x2 -> x0, waiting for transfers between devices: 115 us -> none  [the longest x1 87.2 us: per_device(): lax.psum_scatter(partial_sums.reshape(-1, feature_dim), 'col', scatter_di...]
    pallas_call x0 -> x5, Pallas kernels: none -> 105 us  [the longest x1 62.4 us: layer_call(): pl.pallas_call(functools.partial(layer_kernel, far, near), out_shape=(jax...]
    psum x1, waiting for transfers between devices: 0.02 us -> 103 us  [per_device(): lax.psum(grads, ('row', 'col')) * (1.0 / math.sqrt(rows * n_row * n_col))]
    all_gather x2 -> x0, waiting for transfers between devices: 64.1 us -> none  [the longest x1 47.1 us: spread_back(): row_nodes = lax.all_gather(dscaled, 'col', axis=0, tiled=True)]
    dot_general x22 -> x0, matrix products: 51.2 us -> none  [the longest x8 23.1 us: backward_round(): jnp.einsum('bqc,bqf->bcf', pattern, row_tiles[rows_here], preferred_eleme...]
    reduce_sum x16 -> x0, other arithmetic: 46.8 us -> none  [tile_masks(): multiplicity = jnp.sum(matches.astype(jnp.float32), axis=0)]
    gather x16 -> x0, local copies, waits for them, and re-layouts: 34.3 us -> none  [the longest x8 28.9 us: backward_round(): row_tiles[rows_here]]
  transfers between devices with their start and end apart: 5 -> 1, of which waited for: 4 -> 1; matrix products, arithmetic and copies ran while one was open for 30% -> 0% of each run, Pallas kernels for 0% -> 8%
where the time goes in v1:
time: 234 us
  Pallas kernels  105 us (45%)
  waiting for transfers between devices  103 us (44%)
  between operations  14.8 us (6%)
  local copies, waits for them, and re-layouts  7.59 us (3%)
  other arithmetic  2.92 us (1%)
    psum x1, waiting for transfers between devices, per_device(): lax.psum(grads, ('row', 'col')) * (1.0 / math.sqrt(rows * n_row * n_col))  103 us
    pallas_call x1, Pallas kernels, layer_call(): pl.pallas_call(functools.partial(layer_kernel, far, near), out_shape=(jax...  62.4 us
    pallas_call x2, Pallas kernels, spread(): pl.pallas_call(functools.partial(spread_kernel, forward), out_shape=jax.S...  23 us
    pallas_call x1, Pallas kernels, gather_rows(): pl.pallas_call(functools.partial(gather_rows_kernel, n_row), out_shape=ja...  11.2 us
    pallas_call x1, Pallas kernels, scatter_rows(): pl.pallas_call(functools.partial(scatter_rows_kernel, n_row), out_shape=j...  8.9 us
    unnamed x22, local copies, waits for them, and re-layouts  6.62 us
  transfers between devices with their start and end apart: 1, of which 1 were waited for; matrix products, arithmetic and copies ran while one was open for 0% of the time, Pallas kernels for 8%

profile of v1, /device:TPU:0, one launch (start us, length us, event | category | flops | bytes accessed | tf_op | source)
XLA Modules:
  0.0 234.3 jit_solution(8073821237021715294)
XLA Ops:
  7.2 0.0 copy-start.9
  7.2 0.0 copy-start.8
  7.2 0.0 all-reduce.2.cloned.1.call-start
  7.9 0.7 convert_element_type.3
  8.6 0.1 copy.13.degree_ref
  8.7 0.0 copy-start.1
  8.7 0.9 copy-done.1
  9.7 11.2 %gather_rows.1 = bf16[4,512,256]{2,1,0:T(8,128)(2,1)S(1)} custom-call(bf16[512,256]{1,0:T(8,128)(2,1)S(1)} %copy-done.1), custom_call_target="tpu_custom_call" | custom-call | tf_op jit(solution)/shard_map/gather_rows/pallas_call | solution.py:105
  20.8 1.1 broadcast_select_fusion.edges_ref
  22.0 0.0 copy-done.9
  22.0 0.0 copy-done.8
  22.0 0.0 copy-start.2
  22.0 0.0 copy-start.3
  22.0 0.0 copy-start.4
  22.1 0.0 copy-start.5
  22.1 12.4 %spread_forward.1 = bf16[32,128,256]{2,1,0:T(8,128)(2,1)S(1)} custom-call(s32[256]{0:T(256)S(1)} %copy-done.8, s32[256]{0:T(256)S(1)} %copy-done.9, s32[1]{0:T(128)} %copy.17.count_ref, s32[4,256,128]{2,1,0:T(8,128)S(1)} %broadcast_select_fusion.edges_ref, bf16[16,128,256]{2,1,0:T(8,128)(2,1)S(1)} %bitcast.13), custom_call_target="tpu_custom_call" | custom-call | flops 2147483648 | bytes 3670016 | tf_op jit(solution)/shard_map/spread_forward/pallas_call | solution.py:188
  34.5 0.0 copy-start
  34.5 1.3 copy-done
  35.8 0.0 copy-done.2
  35.8 0.0 copy-done.4
  35.8 62.4 %layer.1 = (bf16[512,256]{1,0:T(8,128)(2,1)S(1)}, f32[512,256]{1,0:T(8,128)S(1)}, f32[2,256,256]{2,1,0:T(8,128)}, bf16[8,512,256]{2,1,0:T(8,128)(2,1)S(1)}) custom-call(bf16[8,512,256]{2,1,0:T(8,128)(2,1)} %bitcast.11, bf16[512,256]{1,0:T(8,128)(2,1)S(1)} %copy-done.2, bf16[256,256]{1,0:T(8,128)(2,1)S(1)} %copy-done.4, bf16[256,256]{1,0:T(8,128)(2,1)S(1)} %copy-done.5, ...), custom_call_target="tpu_custom_call" | custom-call | tf_op jit(solution)/shard_map/layer/pallas_call | solution.py:442
  98.3 0.0 copy-start.6
  98.3 1.3 copy-done.6
  99.6 0.0 all-reduce.2.cloned.1.call-update
  99.6 1.6 copy-done.7
  101.2 10.6 %spread_back.1 = bf16[16,128,256]{2,1,0:T(8,128)(2,1)S(1)} custom-call(s32[256]{0:T(256)S(1)} %copy-done.8, s32[256]{0:T(256)S(1)} %copy-done.9, s32[1]{0:T(128)} %copy.17.count_ref, s32[4,256,128]{2,1,0:T(8,128)S(1)} %broadcast_select_fusion.edges_ref, bf16[32,128,256]{2,1,0:T(8,128)(2,1)S(1)} %bitcast.14), custom_call_target="tpu_custom_call" | custom-call | flops 2147483648 | bytes 3670016 | tf_op jit(solution)/shard_map/spread_back/pallas_call | solution.py:188
  111.8 8.9 %scatter_rows.1 = bf16[512,256]{1,0:T(8,128)(2,1)S(1)} custom-call(bf16[4,512,256]{2,1,0:T(8,128)(2,1)S(1)} %bitcast.12, f32[512,256]{1,0:T(8,128)S(1)} %get-tuple-element.10.own_ref), custom_call_target="tpu_custom_call" | custom-call | tf_op jit(solution)/shard_map/scatter_rows/pallas_call | solution.py:542
  120.7 103.5 %all-reduce.2.cloned.1.call-done = f32[2,256,256]{2,1,0:T(8,128)} async-done(((f32[2,256,256]{2,1,0:T(8,128)}), f32[2,256,256]{2,1,0:T(8,128)}) %all-reduce.2.cloned.1.call-update) | async-done | bytes 524304 | tf_op jit(solution)/shard_map/psum | solution.py:596
  224.1 1.1 broadcast_multiply_fusion
  225.2 0.8 slice_bitcast_fusion
  226.1 0.7 copy.18
  226.8 0.7 copy.19
  (4 shorter events, 0.0 us)
Async XLA Ops:
  7.2 14.8 %copy-start.9 = (s32[256]{0:T(256)S(1)}, s32[256]{0:T(256)}, u32[]{:S(2)}) copy-start(s32[256]{0:T(256)} %cols_ref.3) | copy-start | bytes 3076
  7.2 14.8 %copy-start.8 = (s32[256]{0:T(256)S(1)}, s32[256]{0:T(256)}, u32[]{:S(2)}) copy-start(s32[256]{0:T(256)} %rows_ref.3) | copy-start | bytes 3076
  7.2 217.0 %all-reduce.2.cloned.1.call-start = ((), (), s32[]{:S(2)}) async-start(), calls=%async_computation | async-start | bytes 1048576 | tf_op jit(solution)/shard_map/psum | solution.py:596
  8.7 1.0 copy-start.1
  22.0 13.8 %copy-start.2 = (bf16[512,256]{1,0:T(8,128)(2,1)S(1)}, bf16[512,256]{1,0:T(8,128)(2,1)}, u32[]{:S(2)}) copy-start(bf16[512,256]{1,0:T(8,128)(2,1)} %feat_ref.1) | copy-start | bytes 786436
  22.0 13.8 %copy-start.3 = (bf16[512,256]{1,0:T(8,128)(2,1)S(1)}, bf16[512,256]{1,0:T(8,128)(2,1)}, u32[]{:S(2)}) copy-start(bf16[512,256]{1,0:T(8,128)(2,1)} %cot_ref.1) | copy-start | bytes 786436
  22.0 13.8 %copy-start.4 = (bf16[256,256]{1,0:T(8,128)(2,1)S(1)}, bf16[256,256]{1,0:T(8,128)(2,1)}, u32[]{:S(2)}) copy-start(bf16[256,256]{1,0:T(8,128)(2,1)} %w_self_ref.1) | copy-start | bytes 393220
  22.1 13.8 %copy-start.5 = (bf16[256,256]{1,0:T(8,128)(2,1)S(1)}, bf16[256,256]{1,0:T(8,128)(2,1)}, u32[]{:S(2)}) copy-start(bf16[256,256]{1,0:T(8,128)(2,1)} %w_neigh_ref.1) | copy-start | bytes 393220
  34.5 1.3 copy-start
  98.3 1.3 copy-start.6
  99.6 1.6 copy-start.7
Sparse Core Ops, SparseCore 0:
  99.8 124.3 all-reduce.1
